TPU v7x, 256 devices: a whole 4x4x8 slice. The times are simulated.
256 devices in a mesh: pair: 64 (over x, z_hi, y, core), virt: 4 (over z_lo).
Axes of the slice: x: 4, y: 4, z: 8 (z_hi: 2, z_lo: 4; z = z_hi * 4 + z_lo), core: 2. Of those that a mesh axis runs over, the one named last changes fastest.
Arguments:
- amplitudes: bfloat16 [128, 128, 8, 4096], P('pair', None, 'virt'), may hold values from -6 to 6
- integrals: bfloat16 [8, 4096, 512], P('virt', 'pair'), may hold values from -0.0546875 to 0.0546875
- screen: int32 [128, 8], P('pair', 'virt'), may hold values 0 or 1
- irreps: int32 [16], replicated, may hold values from 0 to 1
- slab_index: int32 [9, 2], replicated, may hold values from 0 to 15, as said below
Outputs:
- ladder: bfloat16 [128, 128, 512], P('pair', None, 'virt')
Inputs may be any that keep to these rules, and one draw needn't show every extreme that they name: `slab_index`: rows 2m + 1 and 2m + 2 name the same two tiles in opposite order, so that contraction tile pair k XOR 1 is the mirror of k.
All inputs are finite; a program needn't handle non-finite values. No bound on the sum of `screen` on one device may be relied on, other than what follows from the above.
Results may differ from a plain program's by a relative error of at most 0.00105.
Values may be sent and summed in bfloat16 or wider, within the bound.
A program may use at most 128 MiB of HBM per device.

v0:
```python
import jax
import jax.numpy as jnp
import numpy as np
from jax import lax
from jax.sharding import PartitionSpec as P

TILE = 64


def body(amplitudes, integrals, screen, irreps, slab_index):
    occ_dev, occupied, local_panels, cell_count = amplitudes.shape
    row_count = occ_dev * occupied
    first_panel = lax.axis_index("virt") * local_panels
    labels = irreps[slab_index]
    local_labels = lax.dynamic_slice_in_dim(labels, first_panel + 1, local_panels, 0)
    parity = (local_labels[:, 0] + local_labels[:, 1] + labels[0, 0] + labels[0, 1]) % 2
    allowed = (parity == 0).astype(jnp.bfloat16)
    partner_order = np.arange(local_panels) ^ 1
    gate_plain = screen.astype(jnp.bfloat16) * allowed[None, :]
    gate_flip = screen[:, partner_order].astype(jnp.bfloat16) * allowed[None, :]
    plain_rows = (amplitudes * gate_plain[:, None, :, None]).reshape(
        row_count, local_panels, cell_count
    )
    plain_major = plain_rows.transpose(1, 2, 0)
    flip_rows = amplitudes[:, :, partner_order] * gate_flip[:, None, :, None]
    flip_rows = flip_rows.reshape(row_count, local_panels, TILE, TILE)
    flip_major = flip_rows.transpose(1, 3, 2, 0).reshape(local_panels, cell_count, row_count)
    stacked = jnp.concatenate([plain_major, flip_major], axis=2)
    columns = integrals.shape[2]
    product = lax.dot_general(
        stacked,
        lax.all_gather(integrals, "pair", axis=1, tiled=True),
        (((0, 1), (0, 1)), ((), ())),
        preferred_element_type=jnp.float32,
    )
    product = product.reshape(2, occ_dev, occupied, columns)
    direct = product[0]
    mirror = product[1]
    direct_sum, mirror_sum = (
        lax.psum_scatter(direct, "virt", scatter_dimension=2, tiled=True),
        lax.psum_scatter(mirror, "virt", scatter_dimension=2, tiled=True),
    )
    mirrored = lax.all_to_all(mirror_sum, "pair", split_axis=1, concat_axis=0, tiled=True)
    result = 0.5 * (direct_sum + mirrored.swapaxes(0, 1))
    return result.astype(jnp.bfloat16)


def solution(mesh):
    in_specs = (P("pair", None, "virt", None), P("virt", "pair", None), P("pair", "virt"), P(), P())
    out_specs = P("pair", None, "virt")
    return jax.shard_map(body, mesh=mesh, in_specs=in_specs, out_specs=out_specs, check_vma=False)
```

profile of v0, /device:TPU:33, one launch (start us, length us, event | category | flops | bytes accessed | tf_op | source)
XLA Modules:
  0.0 257.5 jit_solution(8348305736617038394)
XLA Ops:
  6.5 0.0 copy-start
  6.5 0.0 all-gather.2.cloned.1.call-start
  6.5 0.7 all-gather.2.cloned.1.call-update
  7.3 0.0 reduce-scatter.7.cloned.1.call-start
  7.3 0.8 copy.38
  8.1 0.7 compare_select_fusion
  8.8 0.1 copy.33
  8.9 0.1 reshape.63
  8.9 0.0 copy-done
  9.0 0.0 copy-start.4
  9.0 0.0 copy-start.3
  9.0 0.7 gather_fusion
  9.7 0.1 reshape.62
  9.8 0.0 copy-done.4
  9.8 0.6 gather_fusion.1
  10.4 0.7 fusion.11
  11.0 1.5 add_reduce_fusion
  12.5 0.0 copy-done.3
  12.5 0.1 convert_multiply_fusion
  12.6 0.1 broadcast_bitcast_fusion
  12.7 5.8 %broadcast_multiply_fusion = bf16[2,128,2,4096]{3,2,1,0:T(2,128)(2,1)S(1)} fusion(bf16[2,128,2,4096]{3,2,1,0:T(2,128)(2,1)} %param.8, bf16[2,2]{1,0:T(2,128)(2,1)S(1)} %get-tuple-element.11), kind=kLoop, calls=%fused_computation.10 | loop fusion | flops 2097152 | bytes 8388616 | tf_op jit(solution)/shard_map/mul | solution.py:21
  18.5 0.0 copy-start.2
  18.5 4.9 %copy.34 = bf16[2,128,2,4096]{3,1,0,2:T(8,128)(2,1)} copy(bf16[2,128,2,4096]{3,2,1,0:T(2,128)(2,1)S(1)} %broadcast_multiply_fusion) | data formatting | bytes 8388608 | tf_op jit(solution)/shard_map/mul | solution.py:21
  23.4 0.0 copy-done.2
  23.4 4.6 %fusion.9 = (bf16[2,128,2,2048]{3,2,1,0:T(2,128)(2,1)S(1)}, bf16[2,128,2,2048]{3,2,1,0:T(2,128)(2,1)}) fusion(bf16[2,128,2,4096]{3,2,1,0:T(2,128)(2,1)S(1)} %copy-done.2), kind=kLoop, calls=%fused_computation.28 | loop fusion | bytes 8388608 | tf_op jit(solution)/shard_map/gather | solution.py:25
  28.0 0.9 copy.46
  28.9 2.0 gather_fusion.2
  30.9 2.5 copy.47
  33.4 2.0 gather_fusion.3
  35.4 4.6 %pad_maximum_fusion = bf16[2,128,2,4096]{3,1,0,2:T(8,128)(2,1)} fusion(bf16[2,128,2,2048]{3,1,0,2:T(8,128)(2,1)} %bitcast.39, bf16[2,128,2,2048]{3,1,0,2:T(8,128)(2,1)} %bitcast.38), kind=kLoop, calls=%fused_computation.8 | loop fusion | flops 8388608 | bytes 8388608
  40.0 11.2 %copy.37 = bf16[2,128,2,4096]{1,0,3,2:T(2,128)(2,1)} copy(bf16[2,128,2,4096]{3,1,0,2:T(8,128)(2,1)} %pad_maximum_fusion) | data formatting | bytes 8388608
  51.2 7.6 %gather.13 = bf16[256,2,64,64]{0,3,2,1:T(8,128)(2,1)} reshape(bf16[2,128,2,4096]{1,0,3,2:T(2,128)(2,1)} %copy.37) | data formatting | bytes 8388608 | tf_op jit(solution)/shard_map/gather | solution.py:25
  58.8 2.5 multiply_bitcast_fusion
  61.3 4.4 %copy.39 = bf16[2,64,64,256]{3,2,1,0:T(8,128)(2,1)} copy(bf16[2,64,64,256]{3,1,2,0:T(8,128)(2,1)S(1)} %multiply_bitcast_fusion) | data formatting | bytes 8388608 | tf_op jit(solution)/shard_map/transpose | solution.py:27
  65.7 6.4 %copy.40 = bf16[2,4096,256]{1,2,0:T(8,128)(2,1)} copy(bf16[2,4096,256]{2,1,0:T(8,128)(2,1)} %bitcast.37) | data formatting | bytes 8388608 | tf_op jit(solution)/shard_map/reshape | solution.py:27
  72.1 54.7 %all-gather.2.cloned.1.call-done = bf16[2,4096,512]{2,1,0:T(8,128)(2,1)} async-done(((bf16[2,64,512]{2,1,0:T(8,128)(2,1)}), bf16[2,4096,512]{2,1,0:T(8,128)(2,1)}) %all-gather.2.cloned.1.call-update) | async-done | bytes 8388624 | tf_op jit(solution)/shard_map/all_gather | solution.py:32
  126.7 10.3 %fusion.4 = f32[512,512]{1,0:T(8,128)S(1)} fusion(bf16[2,4096,512]{2,1,0:T(8,128)(2,1)} %all-gather.2.cloned.1.call-done, bf16[2,4096,256]{1,2,0:T(8,128)(2,1)} %copy.40, bf16[2,4096,256]{1,2,0:T(8,128)(2,1)} %bitcast.40), kind=kOutput, calls=%fused_computation.11 | convolution fusion | flops 4311744512 | bytes 17825792 | tf_op jit(solution)/shard_map/dot_general | solution.py:30
  137.1 0.9 fusion.10
  138.0 26.1 %copy.43 = f32[2,128,512]{0,1,2:T(8,128)} copy(f32[2,128,512]{2,1,0:T(8,128)S(1)} %bitcast.41) | data formatting | bytes 1048576
  164.0 24.6 %reshape.96 = f32[512,256]{1,0:T(8,128)} reshape(f32[512,128,2]{2,1,0:T(8,128)} %bitcast.35) | data formatting | bytes 1048576
  188.6 0.0 reduce-scatter.7.cloned.1.call-update
  188.6 0.0 reduce-scatter.5.cloned.1.call-start
  188.7 0.7 reduce-scatter.5.cloned.1.call-update
  189.4 16.4 %reduce-scatter.7.cloned.1.call-done = f32[128,256]{1,0:T(8,128)} async-done(((f32[512,256]{1,0:T(8,128)}), f32[128,256]{1,0:T(8,128)}) %reduce-scatter.7.cloned.1.call-update) | async-done | bytes 131088
  205.7 10.5 %reshape.97 = f32[128,128,2]{2,1,0:T(8,128)} reshape(f32[128,256]{1,0:T(8,128)} %reduce-scatter.7.cloned.1.call-done) | data formatting | bytes 262144
  216.2 0.0 copy-start.1
  216.2 6.6 %copy.44 = f32[2,128,128]{2,0,1:T(2,128)S(1)} copy(f32[2,128,128]{0,1,2:T(8,128)} %bitcast.36) | data formatting | bytes 262144
  222.8 26.4 %all_to_all.18 = f32[2,128,128]{2,0,1:T(2,128)S(1)} all-to-all(f32[2,128,128]{2,0,1:T(2,128)S(1)} %copy.44), channel_id=1, replica_groups=mesh['pair'=64,'virt'=4] {'pair'}, dimensions={1} | all-to-all | bytes 262144 | tf_op jit(solution)/shard_map/all_to_all | solution.py:43
  249.3 0.0 reduce-scatter.5.cloned.1.call-done
  249.4 1.6 multiply_convert_fusion
  250.9 0.0 copy-done.1
  (6 shorter events, 0.1 us)
Async XLA Ops:
  6.5 2.4 copy-start
  6.5 120.2 %all-gather.2.cloned.1.call-start = ((), (), s32[]{:S(2)}) async-start(), calls=%async_computation.3 | async-start | bytes 8519680 | tf_op jit(solution)/shard_map/all_gather | solution.py:32
  7.3 198.5 %reduce-scatter.7.cloned.1.call-start = ((), (), s32[]{:S(2)}) async-start(), calls=%async_computation.5 | async-start | bytes 655360
  9.0 0.8 copy-start.4
  9.0 3.6 %copy-start.3 = (s32[2,2]{1,0:T(2,128)S(1)}, s32[2,2]{1,0:T(2,128)}, u32[]{:S(2)}) copy-start(s32[2,2]{1,0:T(2,128)} %param.10) | copy-start | bytes 52
  18.5 4.9 %copy-start.2 = (bf16[2,128,2,4096]{3,2,1,0:T(2,128)(2,1)S(1)}, bf16[2,128,2,4096]{3,2,1,0:T(2,128)(2,1)}, u32[]{:S(2)}) copy-start(bf16[2,128,2,4096]{3,2,1,0:T(2,128)(2,1)} %param.8) | copy-start | bytes 12582916
  188.6 60.7 %reduce-scatter.5.cloned.1.call-start = ((), (), s32[]{:S(2)}) async-start(), calls=%async_computation.4 | async-start | bytes 655360 | tf_op jit(solution)/shard_map/reduce_scatter | solution.py:40
  216.2 34.7 %copy-start.1 = (s32[16]{0:T(128)S(1)}, s32[16]{0:T(128)}, u32[]{:S(2)}) copy-start(s32[16]{0:T(128)} %param.11) | copy-start | bytes 196
Sparse Core Ops, SparseCore 0:
  11.1 115.5 all-gather.1
  188.7 16.9 reduce-scatter.6
  208.3 25.2 reduce-scatter.4
where the time goes:
time: 260 us; the launch traced here: 257 us
  local copies, waits for them, and re-layouts  118 us (45%)
  waiting for transfers between devices  72.5 us (28%)
  blocking collectives  26.4 us (10%)
  other arithmetic  16.7 us (6%)
  between operations  13.2 us (5%)
  matrix products  10.3 us (4%)
    unnamed x20, local copies, waits for them, and re-layouts  83.2 us
    all_gather x1, waiting for transfers between devices, body(): lax.all_gather(integrals, 'pair', axis=1, tiled=True)  54.7 us
    all_to_all x1, blocking collectives, body(): lax.all_to_all(mirror_sum, 'pair', split_axis=1, concat_axis=0, tiled=True)  26.4 us
    unnamed x4, waiting for transfers between devices  17.8 us
    gather x4, local copies, waits for them, and re-layouts, body(): flip_rows = amplitudes[:, :, partner_order] * gate_flip[:, None, :, None]  16.3 us
    dot_general x1, matrix products, body(): lax.dot_general(stacked, lax.all_gather(integrals, 'pair', axis=1, tiled=...  10.3 us
    reshape x1, local copies, waits for them, and re-layouts, body(): flip_rows.transpose(1, 3, 2, 0).reshape(local_panels, cell_count, row_count)  6.4 us
    mul x1, other arithmetic, body(): amplitudes * gate_plain[:, None, :, None]  5.76 us
  transfers between devices with their start and end apart: 3, of which 2 were waited for; matrix products, arithmetic and copies ran while one was open for 32% of the time, Pallas kernels for 0%

commit v1 on v0

v1 whole, which is shorter than its diff:
```python
import jax
import jax.numpy as jnp
from jax import lax
from jax.experimental import pallas as pl
from jax.experimental.pallas import tpu as pltpu
from jax.sharding import PartitionSpec as P

TILE = 64
STAGES = 4
LANES = 128
MESH = pl.DeviceIdType.MESH

RING1, RING1_FAR, RING2, RING2_FAR, CROSS = 0, 2, 4, 12, 14
COPIES = 18


def pair_index(x, h, y, core):
    return ((x * 2 + h) * 4 + y) * 2 + core


def kernel(
    slab_ref, irreps_ref, screen_ref, own_ref, other_ref, amp_ref, out_ref,
    panels, plain, flipped, turned, partial, arrived, mirror_sum, tiles_out, tiles_in, result,
    local_sem, amp_sem, send_sem, recv_sem, sum_send, sum_recv, tile_send, tile_recv,
):
    pair = lax.axis_index("pair")
    virt = lax.axis_index("virt")
    core = lax.rem(pair, 2)
    y = lax.rem(pair // 2, 4)
    h = lax.rem(pair // 8, 2)
    x = pair // 16
    first = x * (1 - core) + y * core
    second = y * (1 - core) + x * core

    def at(first_pos, second_pos, which_core):
        px = first_pos * (1 - core) + second_pos * core
        py = second_pos * (1 - core) + first_pos * core
        return (pair_index(px, h, py, which_core), virt)

    def around(position, step):
        return lax.rem(position + step, 4)

    first_up, first_down = around(first, 1), around(first, 3)
    second_up, second_down = around(second, 1), around(second, 3)
    first_far, second_far = around(first, 2), around(second, 2)
    blocks = (3 * (1 - virt // 2), lax.rem(2 + 3 * virt, 5), 1 + lax.rem(virt, 2), virt)

    loads = {}
    for panel in range(2):
        for i in range(2):
            loads[panel, i] = pltpu.make_async_copy(
                amp_ref.at[panel, i], plain.at[panel, i], amp_sem.at[panel * 2 + i]
            )
    local = {}
    for q in range(STAGES):
        columns = pl.ds(pl.multiple_of(blocks[q] * LANES, LANES), LANES)
        for n, (ref, level) in enumerate(((own_ref, h), (other_ref, 1 - h))):
            local[q, n] = pltpu.make_async_copy(
                ref.at[:, :, columns],
                panels.at[q, core, second, first, level],
                local_sem.at[q * 2 + n],
            )
            local[q, n].start()
    for load in loads.values():
        load.start()

    barrier = pltpu.get_barrier_semaphore()

    def greet(step, carry):
        pl.semaphore_signal(
            barrier, inc=1, device_id=(lax.rem(pair + step, 64), virt), device_id_type=MESH
        )
        return carry

    lax.fori_loop(1, 64, greet, 0)
    for step in range(1, 4):
        pl.semaphore_signal(
            barrier, inc=1, device_id=(pair, lax.rem(virt + step, 4)), device_id_type=MESH
        )
    pl.semaphore_wait(barrier, 66)

    sent = []

    def block(q, first_pos, second_pos):
        return panels.at[q, core, second_pos, first_pos]

    def half(q, first_pos, second_pos, level):
        return panels.at[q, core, second_pos, first_pos, level]

    def column(q, second_pos):
        return panels.at[q, core, second_pos]

    def column_half(q, second_pos, level):
        return panels.at[q, core, second_pos, :, level]

    def copy(q, number, ref, device):
        return pltpu.make_async_remote_copy(
            src_ref=ref,
            dst_ref=ref,
            send_sem=send_sem.at[q, number],
            recv_sem=recv_sem.at[q, number],
            device_id=device,
            device_id_type=MESH,
        )

    def send(q, number, ref, device):
        moved = copy(q, number, ref, device)
        moved.start()
        sent.append(moved)

    def receive(q, number, ref):
        copy(q, number, ref, at(first, second, 1 - core)).wait_recv()

    def both_ways(q, slot, first_pos):
        send(q, RING2 + slot * 2, block(q, first_pos, second), at(first, second_up, core))
        send(q, RING2 + slot * 2 + 1, block(q, first_pos, second), at(first, second_down, core))

    def cross(q, number, second_pos):
        send(q, CROSS + number, column(q, second_pos), at(first, second, 1 - core))

    def begin(q):
        local[q, 0].wait()
        local[q, 1].wait()
        send(q, RING1, block(q, first, second), at(first_up, second, core))
        send(q, RING1 + 1, block(q, first, second), at(first_down, second, core))
        both_ways(q, 0, first)

    def near(q):
        receive(q, RING1, block(q, first_down, second))
        send(q, RING1_FAR, half(q, first_down, second, 0), at(first_up, second, core))
        both_ways(q, 1, first_down)
        receive(q, RING1 + 1, block(q, first_up, second))
        send(q, RING1_FAR + 1, half(q, first_up, second, 1), at(first_down, second, core))
        both_ways(q, 2, first_up)

    def far(q):
        receive(q, RING1_FAR, half(q, first_far, second, 0))
        receive(q, RING1_FAR + 1, half(q, first_far, second, 1))
        both_ways(q, 3, first_far)
        cross(q, 0, second)

    def near_columns(q):
        order = (first, first_down, first_up, first_far)
        for way, (source, level, target) in enumerate(
            ((second_down, 0, second_up), (second_up, 1, second_down))
        ):
            for slot in range(4):
                receive(q, RING2 + slot * 2 + way, block(q, order[slot], source))
            send(q, RING2_FAR + way, column_half(q, source, level), at(first, target, core))
            cross(q, 1 + way, source)

    def far_columns(q):
        receive(q, RING2_FAR, column_half(q, second_far, 0))
        receive(q, RING2_FAR + 1, column_half(q, second_far, 1))
        cross(q, 3, second_far)

    def complete(q):
        mine = (second, second_down, second_up, second_far)
        for number in range(4):
            copy(q, CROSS + number, column(q, mine[number]), at(first, second, 1 - core)).wait_recv()

    def label(row, side):
        return irreps_ref[slab_ref[row, side]]

    target_label = label(0, 0) + label(0, 1)

    def gate(panel, i):
        row = virt * 2 + panel + 1
        parity = lax.rem(label(row, 0) + label(row, 1) + target_label, 2)
        return (screen_ref[i, panel] * (1 - parity)).astype(jnp.float32)

    def gate_part(panel, i, start, stop):
        level = gate(panel, i)

        def step(m, carry):
            lanes = pl.ds(pl.multiple_of(m * LANES, LANES), LANES)
            block_rows = plain[panel, i, :, lanes].astype(jnp.float32) * level
            plain[panel, i, :, lanes] = block_rows.astype(jnp.bfloat16)
            turned[lanes, :] = block_rows.T
            return carry

        lax.fori_loop(start, stop, step, 0)

    def flip_part(panel, i, start, stop):
        def step(m, carry):
            even = turned[pl.ds(2 * m, TILE, stride=TILE), :]
            odd = turned[pl.ds(2 * m + 1, TILE, stride=TILE), :]
            lanes = pl.ds(pl.multiple_of(m * LANES, LANES), LANES)
            both = jnp.concatenate([even, odd], axis=0).T
            flipped[1 - panel, i, :, lanes] = both.astype(jnp.bfloat16)
            return carry

        lax.fori_loop(start, stop, step, 0)

    parts = []
    for panel in range(2):
        for i in range(2):
            for start in (0, 16):
                parts.append((gate_part, panel, i, start))
            for start in (0, 16):
                parts.append((flip_part, panel, i, start))
    loaded = set()

    def prepare(count):
        for _ in range(count):
            if not parts:
                return
            part, panel, i, start = parts.pop(0)
            if (panel, i) not in loaded:
                loaded.add((panel, i))
                loads[panel, i].wait()
            part(panel, i, start, start + 16)

    def multiply(q, rows_of):
        for rows in rows_of:
            partial[q, rows] = jnp.zeros((256, LANES), jnp.float32)

        def step(n, carry):
            panel, at_x = n // 4, lax.rem(n, 4)
            cells = []
            for level in range(2):
                for at_y in range(4):
                    cells.append(panels[q, 0, at_y, at_x, level, panel])
                    cells.append(panels[q, 1, at_x, at_y, level, panel])
            right = jnp.concatenate(cells, axis=0)
            lanes = pl.ds(pl.multiple_of(at_x * 1024, 1024), 1024)
            for rows in rows_of:
                source = (plain, flipped)[rows]
                left = source[panel, :, :, lanes].reshape(256, 1024)
                partial[q, rows] += jnp.dot(left, right, preferred_element_type=jnp.float32)
            return carry

        lax.fori_loop(0, 8, step, 0)

    sums = []

    def pass_on(q):
        moved = pltpu.make_async_remote_copy(
            src_ref=partial.at[q],
            dst_ref=arrived.at[virt],
            send_sem=sum_send.at[q],
            recv_sem=sum_recv.at[virt],
            device_id=(pair, blocks[q]),
            device_id_type=MESH,
        )
        moved.start()
        sums.append(moved)

    begin(0)
    begin(1)
    prepare(2)
    near(0)
    prepare(2)
    far(0)
    begin(2)
    near(1)
    prepare(2)
    near_columns(0)
    far(1)
    prepare(2)
    far_columns(0)
    begin(3)
    near(2)
    prepare(2)
    near_columns(1)
    far(2)
    prepare(2)
    far_columns(1)
    near(3)
    prepare(len(parts))
    complete(0)
    multiply(0, (1, 0))
    pass_on(0)
    near_columns(2)
    far(3)
    complete(1)
    multiply(1, (1, 0))
    pass_on(1)
    far_columns(2)
    near_columns(3)
    complete(2)
    multiply(2, (1, 0))
    pass_on(2)
    far_columns(3)
    complete(3)
    multiply(3, (1,))

    others = [lax.rem(virt + step, 4) for step in range(1, 4)]
    for other in others:
        pltpu.make_async_remote_copy(
            src_ref=partial.at[0],
            dst_ref=arrived.at[other],
            send_sem=sum_send.at[0],
            recv_sem=sum_recv.at[other],
            device_id=(pair, other),
            device_id_type=MESH,
        ).wait_recv()
    mirror_sum[...] = partial[3, 1] + (
        arrived[others[0], 1] + arrived[others[1], 1] + arrived[others[2], 1]
    )
    for which in range(2):
        for i in range(2):
            for j in range(2):
                rows = mirror_sum[pl.ds(i * 128 + which * 2 + j, 32, stride=4), :]
                tiles_out[pl.ds(which * 4 + i * 2 + j, 32, stride=8), :] = rows

    def tile_copy(target):
        return pltpu.make_async_remote_copy(
            src_ref=tiles_out.at[pl.ds(pl.multiple_of((target // 2) * 8, 8), 8)],
            dst_ref=tiles_in.at[pl.ds(pl.multiple_of(pair * 8, 8), 8)],
            send_sem=tile_send,
            recv_sem=tile_recv,
            device_id=(target, virt),
            device_id_type=MESH,
        )

    def exchange(step, carry):
        tile_copy(lax.rem(pair + step, 64)).start()
        return carry

    lax.fori_loop(1, 64, exchange, 0)
    tiles_in[pl.ds(pl.multiple_of(pair * 8, 8), 8), :] = tiles_out[
        pl.ds(pl.multiple_of((pair // 2) * 8, 8), 8), :
    ]
    multiply(3, (0,))
    partial[3, 0] += arrived[others[0], 0] + arrived[others[1], 0] + arrived[others[2], 0]

    everything = pltpu.make_async_remote_copy(
        src_ref=tiles_in.at[pl.ds(0, 63 * 8)],
        dst_ref=tiles_in.at[pl.ds(0, 63 * 8)],
        send_sem=tile_send,
        recv_sem=tile_recv,
        device_id=(lax.rem(pair + 1, 64), virt),
        device_id_type=MESH,
    )
    everything.wait_recv()
    for i in range(2):
        for j in range(2):
            direct = partial[3, 0, pl.ds(i * 128 + j, 64, stride=2), :]
            mirrored = tiles_in[pl.ds(core * 4 + j * 2 + i, 64, stride=8), :]
            result[pl.ds(i * 128 + j, 64, stride=2), :] = 0.5 * (direct + mirrored)
    out_ref[...] = result[...].astype(jnp.bfloat16).reshape(2, 128, LANES)

    everything.wait_send()
    for moved in sums:
        moved.wait_send()
    for moved in sent:
        moved.wait_send()


def body(amplitudes, integrals, screen, irreps, slab_index):
    swap = [(p, p ^ 8) for p in range(64)]
    other = lax.ppermute(integrals, "pair", swap)
    rows = amplitudes.transpose(2, 0, 1, 3)
    smem = pl.BlockSpec(memory_space=pltpu.SMEM)
    anywhere = pl.BlockSpec(memory_space=pl.ANY)
    vmem = pl.BlockSpec(memory_space=pltpu.VMEM)
    dma, f32, bf16 = pltpu.SemaphoreType.DMA, jnp.float32, jnp.bfloat16
    return pl.pallas_call(
        kernel,
        out_shape=jax.ShapeDtypeStruct((2, 128, LANES), bf16),
        in_specs=[smem, smem, smem, anywhere, anywhere, anywhere],
        out_specs=vmem,
        scratch_shapes=[
            pltpu.VMEM((STAGES, 2, 4, 4, 2, 2, TILE, LANES), bf16),
            pltpu.VMEM((2, 2, 128, 4096), bf16),
            pltpu.VMEM((2, 2, 128, 4096), bf16),
            pltpu.VMEM((4096, 128), f32),
            pltpu.VMEM((STAGES, 2, 256, LANES), f32),
            pltpu.VMEM((4, 2, 256, LANES), f32),
            pltpu.VMEM((256, LANES), f32),
            pltpu.VMEM((32 * 8, LANES), f32),
            pltpu.VMEM((64 * 8, LANES), f32),
            pltpu.VMEM((256, LANES), f32),
            dma((STAGES * 2,)),
            dma((4,)),
            dma((STAGES, COPIES)),
            dma((STAGES, COPIES)),
            dma((STAGES,)),
            dma((4,)),
            dma,
            dma,
        ],
        compiler_params=pltpu.CompilerParams(
            collective_id=0, has_side_effects=True, vmem_limit_bytes=40 * 1024 * 1024
        ),
        cost_estimate=pl.CostEstimate(
            flops=2 * 512 * 8192 * 512, bytes_accessed=5 << 20, transcendentals=0
        ),
    )(slab_index, irreps, screen, integrals, other, rows)


def solution(mesh):
    in_specs = (P("pair", None, "virt", None), P("virt", "pair", None), P("pair", "virt"), P(), P())
    out_specs = P("pair", None, "virt")
    return jax.shard_map(body, mesh=mesh, in_specs=in_specs, out_specs=out_specs, check_vma=False)
```

time: 260 us -> 92.7 us (0.36)
  local copies, waits for them, and re-layouts: 118 us -> 6.54 us
  Pallas kernels: 0 us -> 80 us
  waiting for transfers between devices: 72.5 us -> 0.01 us
  blocking collectives: 26.4 us -> 0 us
  other arithmetic: 16.7 us -> 0 us
  between operations: 13.2 us -> 0.05 us
  matrix products: 10.3 us -> 0 us
  starting transfers between devices: 0.08 us -> 6.01 us
    pallas_call x0 -> x1, Pallas kernels: none -> 80 us  [body(): pl.pallas_call(kernel, out_shape=jax.ShapeDtypeStruct((2, 128, LANES), bf...]
    unnamed x20 -> x9, local copies, waits for them, and re-layouts: 83.2 us -> 6.54 us
    all_gather x1 -> x0, waiting for transfers between devices: 54.7 us -> none  [body(): lax.all_gather(integrals, 'pair', axis=1, tiled=True)]
    all_to_all x1 -> x0, blocking collectives: 26.4 us -> none  [body(): lax.all_to_all(mirror_sum, 'pair', split_axis=1, concat_axis=0, tiled=True)]
    unnamed x4 -> x0, waiting for transfers between devices: 17.8 us -> none
    gather x7 -> x0, local copies, waits for them, and re-layouts: 17.6 us -> none  [the longest x4 16.3 us: body(): flip_rows = amplitudes[:, :, partner_order] * gate_flip[:, None, :, None]]
    dot_general x1 -> x0, matrix products: 10.3 us -> none  [body(): lax.dot_general(stacked, lax.all_gather(integrals, 'pair', axis=1, tiled=...]
    reshape x1 -> x0, local copies, waits for them, and re-layouts: 6.4 us -> none  [body(): flip_rows.transpose(1, 3, 2, 0).reshape(local_panels, cell_count, row_count)]
  transfers between devices with their start and end apart: 3 -> 1, of which waited for: 2 -> 0; matrix products, arithmetic and copies ran while one was open for 32% -> 6% of each run, Pallas kernels for 0% -> 0%
where the time goes in v1:
time: 92.7 us; the launch traced here: 92.6 us
  Pallas kernels  80 us (86%)
  local copies, waits for them, and re-layouts  6.54 us (7%)
  starting transfers between devices  6.01 us (6%)
    pallas_call x1, Pallas kernels, body(): pl.pallas_call(kernel, out_shape=jax.ShapeDtypeStruct((2, 128, LANES), bf...  80 us
    unnamed x9, local copies, waits for them, and re-layouts  6.54 us
    ppermute x1, starting transfers between devices, body(): other = lax.ppermute(integrals, 'pair', swap)  6.01 us
  transfers between devices with their start and end apart: 1, of which 0 were waited for; matrix products, arithmetic and copies ran while one was open for 6% of the time, Pallas kernels for 0%

profile of v1, /device:TPU:33, one launch (start us, length us, event | category | flops | bytes accessed | tf_op | source)
XLA Modules:
  0.0 92.6 jit_solution(14897617202845359225)
XLA Ops:
  0.0 6.0 %collective-permute-start = (bf16[2,64,512]{2,1,0:T(8,128)(2,1)}, bf16[2,64,512]{2,1,0:T(8,128)(2,1)S(1)}, u32[]{:S(2)}, u32[]{:S(2)}) collective-permute-start(bf16[2,64,512]{2,1,0:T(8,128)(2,1)} %own_ref.1), channel_id=1, source_target_pairs={{0,32},{4,36},{8,40},{12,44},{16,48},{20,52},{24,56},{28,60},{32,0... | collective-permute-start | bytes 393224 | tf_op jit(solution)/shard_map/ppermute | solution.py:353
  6.0 0.8 copy.7.slab_ref
  6.8 0.0 copy-start
  6.8 0.0 copy-start.1
  6.8 0.0 copy-start.2
  6.8 5.1 %copy.9 = bf16[2,128,2,4096]{3,1,0,2:T(8,128)(2,1)S(1)} copy(bf16[2,128,2,4096]{3,2,1,0:T(2,128)(2,1)} %param.5) | data formatting | bytes 8388608 | tf_op args[0]
  11.9 0.0 collective-permute-done.other_ref
  11.9 0.0 copy-done
  11.9 0.0 copy-done.1
  11.9 0.0 copy-done.2
  12.0 80.0 %shard_map.55 = bf16[2,128,128]{2,1,0:T(8,128)(2,1)S(1)} custom-call(s32[9,2]{1,0:T(8,128)S(1)} %copy.7.slab_ref, s32[16]{0:T(128)S(1)} %copy-done.2, s32[2,2]{1,0:T(2,128)S(1)} %copy-done.1, bf16[2,64,512]{2,1,0:T(8,128)(2,1)S(1)} %copy-done, bf16[2,64,512]{2,1,0:T(8,128)(2,1)S(1)} %collective-permute-done.other_ref, bf16[2,2,128,4096]{3,2,1,0:T(8,128)(2,1)S(1)} %bitcast.3), custom_call_target="tpu_custom_call" | custom-call | flops 4294967296 | bytes 5242880 | tf_op jit(solution)/shard_map/pallas_call | solution.py:359
  91.9 0.6 copy.11
Async XLA Ops:
  0.0 11.9 %collective-permute-start = (bf16[2,64,512]{2,1,0:T(8,128)(2,1)}, bf16[2,64,512]{2,1,0:T(8,128)(2,1)S(1)}, u32[]{:S(2)}, u32[]{:S(2)}) collective-permute-start(bf16[2,64,512]{2,1,0:T(8,128)(2,1)} %own_ref.1), channel_id=1, source_target_pairs={{0,32},{4,36},{8,40},{12,44},{16,48},{20,52},{24,56},{28,60},{32,0... | collective-permute-start | bytes 393224 | tf_op jit(solution)/shard_map/ppermute | solution.py:353
  6.8 5.2 %copy-start = (bf16[2,64,512]{2,1,0:T(8,128)(2,1)S(1)}, bf16[2,64,512]{2,1,0:T(8,128)(2,1)}, u32[]{:S(2)}) copy-start(bf16[2,64,512]{2,1,0:T(8,128)(2,1)} %own_ref.1) | copy-start | bytes 393220
  6.8 5.2 %copy-start.1 = (s32[2,2]{1,0:T(2,128)S(1)}, s32[2,2]{1,0:T(2,128)}, u32[]{:S(2)}) copy-start(s32[2,2]{1,0:T(2,128)} %screen_ref.1) | copy-start | bytes 52
  6.8 5.2 %copy-start.2 = (s32[16]{0:T(128)S(1)}, s32[16]{0:T(128)}, u32[]{:S(2)}) copy-start(s32[16]{0:T(128)} %irreps_ref.1) | copy-start | bytes 196

commit v2 on v1

--- a/solution.py
+++ b/solution.py
@@ -10,8 +10,9 @@
 LANES = 128
 MESH = pl.DeviceIdType.MESH
 
-RING1, RING1_FAR, RING2, RING2_FAR, CROSS = 0, 2, 4, 12, 14
-COPIES = 18
+RING1, RING1_FAR, RING2, RING2_NEAR, RING2_FAR, ACROSS, CROSS, LEVEL = 0, 4, 6, 10, 12, 14, 16, 20
+COPIES = 21
+OWN, UP, DOWN, FAR = 0, 1, 2, 3
 
 
 def pair_index(x, h, y, core):
@@ -19,7 +20,7 @@
 
 
 def kernel(
-    slab_ref, irreps_ref, screen_ref, own_ref, other_ref, amp_ref, out_ref,
+    slab_ref, irreps_ref, screen_ref, own_ref, amp_ref, out_ref,
     panels, plain, flipped, turned, partial, arrived, mirror_sum, tiles_out, tiles_in, result,
     local_sem, amp_sem, send_sem, recv_sem, sum_send, sum_recv, tile_send, tile_recv,
 ):
@@ -32,17 +33,20 @@
     first = x * (1 - core) + y * core
     second = y * (1 - core) + x * core
 
-    def at(first_pos, second_pos, which_core):
+    def at(first_pos, second_pos, level, which_core):
         px = first_pos * (1 - core) + second_pos * core
         py = second_pos * (1 - core) + first_pos * core
-        return (pair_index(px, h, py, which_core), virt)
+        return (pair_index(px, level, py, which_core), virt)
 
     def around(position, step):
         return lax.rem(position + step, 4)
 
-    first_up, first_down = around(first, 1), around(first, 3)
-    second_up, second_down = around(second, 1), around(second, 3)
-    first_far, second_far = around(first, 2), around(second, 2)
+    first_up = at(around(first, 1), second, h, core)
+    first_down = at(around(first, 3), second, h, core)
+    second_up = at(first, around(second, 1), h, core)
+    second_down = at(first, around(second, 3), h, core)
+    sibling = at(first, second, h, 1 - core)
+    opposite = at(first, second, 1 - h, core)
     blocks = (3 * (1 - virt // 2), lax.rem(2 + 3 * virt, 5), 1 + lax.rem(virt, 2), virt)
 
     loads = {}
@@ -54,110 +58,93 @@
     local = {}
     for q in range(STAGES):
         columns = pl.ds(pl.multiple_of(blocks[q] * LANES, LANES), LANES)
-        for n, (ref, level) in enumerate(((own_ref, h), (other_ref, 1 - h))):
-            local[q, n] = pltpu.make_async_copy(
-                ref.at[:, :, columns],
-                panels.at[q, core, second, first, level],
-                local_sem.at[q * 2 + n],
-            )
-            local[q, n].start()
+        local[q] = pltpu.make_async_copy(
+            own_ref.at[:, :, columns], panels.at[q, core, OWN, OWN, h], local_sem.at[q]
+        )
+        local[q].start()
     for load in loads.values():
         load.start()
 
     barrier = pltpu.get_barrier_semaphore()
-
-    def greet(step, carry):
-        pl.semaphore_signal(
-            barrier, inc=1, device_id=(lax.rem(pair + step, 64), virt), device_id_type=MESH
-        )
-        return carry
-
-    lax.fori_loop(1, 64, greet, 0)
-    for step in range(1, 4):
-        pl.semaphore_signal(
-            barrier, inc=1, device_id=(pair, lax.rem(virt + step, 4)), device_id_type=MESH
-        )
-    pl.semaphore_wait(barrier, 66)
+    along = [(pair, lax.rem(virt + step, 4)) for step in range(1, 4)]
+    for device in [first_up, first_down, second_up, second_down, sibling, opposite] + along:
+        pl.semaphore_signal(barrier, inc=1, device_id=device, device_id_type=MESH)
+    pl.semaphore_wait(barrier, 9)
 
     sent = []
 
-    def block(q, first_pos, second_pos):
-        return panels.at[q, core, second_pos, first_pos]
-
-    def half(q, first_pos, second_pos, level):
-        return panels.at[q, core, second_pos, first_pos, level]
-
-    def column(q, second_pos):
-        return panels.at[q, core, second_pos]
-
-    def column_half(q, second_pos, level):
-        return panels.at[q, core, second_pos, :, level]
-
-    def copy(q, number, ref, device):
+    def copy(q, number, source, target, device):
         return pltpu.make_async_remote_copy(
-            src_ref=ref,
-            dst_ref=ref,
+            src_ref=panels.at[(q, core) + source],
+            dst_ref=panels.at[(q, core) + target],
             send_sem=send_sem.at[q, number],
             recv_sem=recv_sem.at[q, number],
             device_id=device,
             device_id_type=MESH,
         )
 
-    def send(q, number, ref, device):
-        moved = copy(q, number, ref, device)
+    def send(q, number, source, target, device):
+        moved = copy(q, number, source, target, device)
         moved.start()
         sent.append(moved)
 
-    def receive(q, number, ref):
-        copy(q, number, ref, at(first, second, 1 - core)).wait_recv()
-
-    def both_ways(q, slot, first_pos):
-        send(q, RING2 + slot * 2, block(q, first_pos, second), at(first, second_up, core))
-        send(q, RING2 + slot * 2 + 1, block(q, first_pos, second), at(first, second_down, core))
-
-    def cross(q, number, second_pos):
-        send(q, CROSS + number, column(q, second_pos), at(first, second, 1 - core))
+    def receive(q, number, target):
+        copy(q, number, target, target, sibling).wait_recv()
+
+    def start_level(q, which, level):
+        send(q, RING1 + which, (OWN, OWN, level), (OWN, DOWN, level), first_up)
+        send(q, RING1 + which + 2, (OWN, OWN, level), (OWN, UP, level), first_down)
+        send(q, RING2 + which, (OWN, OWN, level), (DOWN, OWN, level), second_up)
+        send(q, RING2 + which + 2, (OWN, OWN, level), (UP, OWN, level), second_down)
 
     def begin(q):
-        local[q, 0].wait()
-        local[q, 1].wait()
-        send(q, RING1, block(q, first, second), at(first_up, second, core))
-        send(q, RING1 + 1, block(q, first, second), at(first_down, second, core))
-        both_ways(q, 0, first)
+        local[q].wait()
+        send(q, LEVEL, (OWN, OWN, h), (OWN, OWN, h), opposite)
+        start_level(q, 0, h)
+
+    def begin_other(q):
+        receive(q, LEVEL, (OWN, OWN, 1 - h))
+        start_level(q, 1, 1 - h)
+
+    near_two = pl.ds(UP, 2)
 
     def near(q):
-        receive(q, RING1, block(q, first_down, second))
-        send(q, RING1_FAR, half(q, first_down, second, 0), at(first_up, second, core))
-        both_ways(q, 1, first_down)
-        receive(q, RING1 + 1, block(q, first_up, second))
-        send(q, RING1_FAR + 1, half(q, first_up, second, 1), at(first_down, second, core))
-        both_ways(q, 2, first_up)
+        for which, level in enumerate((h, 1 - h)):
+            receive(q, RING1 + which, (OWN, DOWN, level))
+            receive(q, RING1 + which + 2, (OWN, UP, level))
+        send(q, RING1_FAR, (OWN, DOWN, h), (OWN, FAR, h), first_up)
+        send(q, RING1_FAR + 1, (OWN, UP, 1 - h), (OWN, FAR, 1 - h), first_down)
+        send(q, RING2_NEAR, (OWN, near_two), (DOWN, near_two), second_up)
+        send(q, RING2_NEAR + 1, (OWN, near_two), (UP, near_two), second_down)
 
     def far(q):
-        receive(q, RING1_FAR, half(q, first_far, second, 0))
-        receive(q, RING1_FAR + 1, half(q, first_far, second, 1))
-        both_ways(q, 3, first_far)
-        cross(q, 0, second)
+        receive(q, RING1_FAR, (OWN, FAR, h))
+        receive(q, RING1_FAR + 1, (OWN, FAR, 1 - h))
+        send(q, RING2_FAR, (OWN, FAR), (DOWN, FAR), second_up)
+        send(q, RING2_FAR + 1, (OWN, FAR), (UP, FAR), second_down)
+        send(q, CROSS, (OWN,), (OWN,), sibling)
+
+    every = pl.ds(0, 4)
 
     def near_columns(q):
-        order = (first, first_down, first_up, first_far)
-        for way, (source, level, target) in enumerate(
-            ((second_down, 0, second_up), (second_up, 1, second_down))
+        for way, (side, level, target) in enumerate(
+            ((DOWN, h, second_up), (UP, 1 - h, second_down))
         ):
-            for slot in range(4):
-                receive(q, RING2 + slot * 2 + way, block(q, order[slot], source))
-            send(q, RING2_FAR + way, column_half(q, source, level), at(first, target, core))
-            cross(q, 1 + way, source)
+            receive(q, RING2 + way * 2, (side, OWN, h))
+            receive(q, RING2 + way * 2 + 1, (side, OWN, 1 - h))
+            receive(q, RING2_NEAR + way, (side, near_two))
+            receive(q, RING2_FAR + way, (side, FAR))
+            send(q, ACROSS + way, (side, every, level), (FAR, every, level), target)
+            send(q, CROSS + 1 + way, (side,), (side,), sibling)
 
     def far_columns(q):
-        receive(q, RING2_FAR, column_half(q, second_far, 0))
-        receive(q, RING2_FAR + 1, column_half(q, second_far, 1))
-        cross(q, 3, second_far)
+        receive(q, ACROSS, (FAR, every, h))
+        receive(q, ACROSS + 1, (FAR, every, 1 - h))
+        send(q, CROSS + 3, (FAR,), (FAR,), sibling)
 
     def complete(q):
-        mine = (second, second_down, second_up, second_far)
         for number in range(4):
-            copy(q, CROSS + number, column(q, mine[number]), at(first, second, 1 - core)).wait_recv()
+            receive(q, CROSS + number, (number,))
 
     def label(row, side):
         return irreps_ref[slab_ref[row, side]]
@@ -169,28 +156,34 @@
         parity = lax.rem(label(row, 0) + label(row, 1) + target_label, 2)
         return (screen_ref[i, panel] * (1 - parity)).astype(jnp.float32)
 
+    def unrolled(one, start, stop):
+        def step(m, carry):
+            for n in range(4):
+                one(m * 4 + n)
+            return carry
+
+        lax.fori_loop(start // 4, stop // 4, step, 0)
+
     def gate_part(panel, i, start, stop):
         level = gate(panel, i)
 
-        def step(m, carry):
+        def one(m):
             lanes = pl.ds(pl.multiple_of(m * LANES, LANES), LANES)
             block_rows = plain[panel, i, :, lanes].astype(jnp.float32) * level
             plain[panel, i, :, lanes] = block_rows.astype(jnp.bfloat16)
             turned[lanes, :] = block_rows.T
-            return carry
-
-        lax.fori_loop(start, stop, step, 0)
+
+        unrolled(one, start, stop)
 
     def flip_part(panel, i, start, stop):
-        def step(m, carry):
+        def one(m):
             even = turned[pl.ds(2 * m, TILE, stride=TILE), :]
             odd = turned[pl.ds(2 * m + 1, TILE, stride=TILE), :]
             lanes = pl.ds(pl.multiple_of(m * LANES, LANES), LANES)
             both = jnp.concatenate([even, odd], axis=0).T
             flipped[1 - panel, i, :, lanes] = both.astype(jnp.bfloat16)
-            return carry
-
-        lax.fori_loop(start, stop, step, 0)
+
+        unrolled(one, start, stop)
 
     parts = []
     for panel in range(2):
@@ -211,6 +204,10 @@
                 loads[panel, i].wait()
             part(panel, i, start, start + 16)
 
+    def place(position, centre):
+        distance = lax.rem(position - centre + 4, 4)
+        return distance + distance // 2 - 2 * (distance // 3)
+
     def multiply(q, rows_of):
         for rows in rows_of:
             partial[q, rows] = jnp.zeros((256, LANES), jnp.float32)
@@ -220,8 +217,9 @@
             cells = []
             for level in range(2):
                 for at_y in range(4):
-                    cells.append(panels[q, 0, at_y, at_x, level, panel])
-                    cells.append(panels[q, 1, at_x, at_y, level, panel])
+                    near_x, near_y = place(at_x, x), place(at_y, y)
+                    cells.append(panels[q, 0, near_y, near_x, level, panel])
+                    cells.append(panels[q, 1, near_x, near_y, level, panel])
             right = jnp.concatenate(cells, axis=0)
             lanes = pl.ds(pl.multiple_of(at_x * 1024, 1024), 1024)
             for rows in rows_of:
@@ -246,20 +244,22 @@
         moved.start()
         sums.append(moved)
 
-    begin(0)
-    begin(1)
-    prepare(2)
+    for q in range(STAGES):
+        begin(q)
+    begin_other(0)
+    prepare(2)
+    begin_other(1)
     near(0)
     prepare(2)
     far(0)
-    begin(2)
+    begin_other(2)
     near(1)
     prepare(2)
+    begin_other(3)
     near_columns(0)
     far(1)
     prepare(2)
     far_columns(0)
-    begin(3)
     near(2)
     prepare(2)
     near_columns(1)
@@ -349,8 +349,6 @@
 
 
 def body(amplitudes, integrals, screen, irreps, slab_index):
-    swap = [(p, p ^ 8) for p in range(64)]
-    other = lax.ppermute(integrals, "pair", swap)
     rows = amplitudes.transpose(2, 0, 1, 3)
     smem = pl.BlockSpec(memory_space=pltpu.SMEM)
     anywhere = pl.BlockSpec(memory_space=pl.ANY)
@@ -359,7 +357,7 @@
     return pl.pallas_call(
         kernel,
         out_shape=jax.ShapeDtypeStruct((2, 128, LANES), bf16),
-        in_specs=[smem, smem, smem, anywhere, anywhere, anywhere],
+        in_specs=[smem, smem, smem, anywhere, anywhere],
         out_specs=vmem,
         scratch_shapes=[
             pltpu.VMEM((STAGES, 2, 4, 4, 2, 2, TILE, LANES), bf16),
@@ -372,7 +370,7 @@
             pltpu.VMEM((32 * 8, LANES), f32),
             pltpu.VMEM((64 * 8, LANES), f32),
             pltpu.VMEM((256, LANES), f32),
-            dma((STAGES * 2,)),
+            dma((STAGES,)),
             dma((4,)),
             dma((STAGES, COPIES)),
             dma((STAGES, COPIES)),
@@ -387,7 +385,7 @@
         cost_estimate=pl.CostEstimate(
             flops=2 * 512 * 8192 * 512, bytes_accessed=5 << 20, transcendentals=0
         ),
-    )(slab_index, irreps, screen, integrals, other, rows)
+    )(slab_index, irreps, screen, integrals, rows)
 
 
 def solution(mesh):

time: 92.7 us -> 83.1 us (0.90)
  starting transfers between devices: 6.01 us -> 0 us
  Pallas kernels: 80 us -> 76.4 us
    ppermute x1 -> x0, starting transfers between devices: 6.01 us -> none  [body(): other = lax.ppermute(integrals, 'pair', swap)]
    pallas_call x1, Pallas kernels: 80 us -> 76.4 us  [body(): pl.pallas_call(kernel, out_shape=jax.ShapeDtypeStruct((2, 128, LANES), bf...]
  transfers between devices with their start and end apart: 1 -> 0, of which waited for: 0 -> 0; matrix products, arithmetic and copies ran while one was open for 6% -> 0% of each run, Pallas kernels for 0% -> 0%
where the time goes in v2:
time: 83.1 us; the launch traced here: 83 us
  Pallas kernels  76.4 us (92%)
  local copies, waits for them, and re-layouts  6.54 us (8%)
    pallas_call x1, Pallas kernels, body(): pl.pallas_call(kernel, out_shape=jax.ShapeDtypeStruct((2, 128, LANES), bf...  76.4 us
    unnamed x9, local copies, waits for them, and re-layouts  6.54 us

profile of v2, /device:TPU:33, one launch (start us, length us, event | category | flops | bytes accessed | tf_op | source)
XLA Modules:
  0.0 83.0 jit_solution(8198738521787942762)
XLA Ops:
  0.0 0.8 copy.7.slab_ref
  0.8 0.0 copy-start
  0.8 0.0 copy-start.1
  0.8 0.0 copy-start.2
  0.8 5.1 %copy.9 = bf16[2,128,2,4096]{3,1,0,2:T(8,128)(2,1)S(1)} copy(bf16[2,128,2,4096]{3,2,1,0:T(2,128)(2,1)} %param.5) | data formatting | bytes 8388608 | tf_op args[0]
  5.9 0.0 copy-done
  5.9 0.0 copy-done.1
  5.9 0.0 copy-done.2
  5.9 76.4 %shard_map.55 = bf16[2,128,128]{2,1,0:T(8,128)(2,1)S(1)} custom-call(s32[9,2]{1,0:T(8,128)S(1)} %copy.7.slab_ref, s32[16]{0:T(128)S(1)} %copy-done.2, s32[2,2]{1,0:T(2,128)S(1)} %copy-done.1, bf16[2,64,512]{2,1,0:T(8,128)(2,1)S(1)} %copy-done, bf16[2,2,128,4096]{3,2,1,0:T(8,128)(2,1)S(1)} %bitcast.3), custom_call_target="tpu_custom_call" | custom-call | flops 4294967296 | bytes 5242880 | tf_op jit(solution)/shard_map/pallas_call | solution.py:357
  82.4 0.6 copy.11
Async XLA Ops:
  0.8 5.1 %copy-start = (bf16[2,64,512]{2,1,0:T(8,128)(2,1)S(1)}, bf16[2,64,512]{2,1,0:T(8,128)(2,1)}, u32[]{:S(2)}) copy-start(bf16[2,64,512]{2,1,0:T(8,128)(2,1)} %own_ref.1) | copy-start | bytes 393220
  0.8 5.2 %copy-start.1 = (s32[2,2]{1,0:T(2,128)S(1)}, s32[2,2]{1,0:T(2,128)}, u32[]{:S(2)}) copy-start(s32[2,2]{1,0:T(2,128)} %screen_ref.1) | copy-start | bytes 52
  0.8 5.2 %copy-start.2 = (s32[16]{0:T(128)S(1)}, s32[16]{0:T(128)}, u32[]{:S(2)}) copy-start(s32[16]{0:T(128)} %irreps_ref.1) | copy-start | bytes 196

commit v3 on v2

--- a/solution.py
+++ b/solution.py
@@ -10,8 +10,9 @@
 LANES = 128
 MESH = pl.DeviceIdType.MESH
 
-RING1, RING1_FAR, RING2, RING2_NEAR, RING2_FAR, ACROSS, CROSS, LEVEL = 0, 4, 6, 10, 12, 14, 16, 20
-COPIES = 21
+RING1, RING2, RING2_REST, ACROSS, CROSS, LEVEL = 0, 6, 10, 14, 16, 19
+COPIES = 20
+STEPS = 32000.0
 OWN, UP, DOWN, FAR = 0, 1, 2, 3
 
 
@@ -21,7 +22,7 @@
 
 def kernel(
     slab_ref, irreps_ref, screen_ref, own_ref, amp_ref, out_ref,
-    panels, plain, flipped, turned, partial, arrived, mirror_sum, tiles_out, tiles_in, result,
+    panels, amps, turned, partial, coded, scales, arrived, arrived_scales, mirror_sum, tiles_out, tiles_in, result,
     local_sem, amp_sem, send_sem, recv_sem, sum_send, sum_recv, tile_send, tile_recv,
 ):
     pair = lax.axis_index("pair")
@@ -43,6 +44,7 @@
 
     first_up = at(around(first, 1), second, h, core)
     first_down = at(around(first, 3), second, h, core)
+    first_far = at(around(first, 2), second, h, core)
     second_up = at(first, around(second, 1), h, core)
     second_down = at(first, around(second, 3), h, core)
     sibling = at(first, second, h, 1 - core)
@@ -53,7 +55,7 @@
     for panel in range(2):
         for i in range(2):
             loads[panel, i] = pltpu.make_async_copy(
-                amp_ref.at[panel, i], plain.at[panel, i], amp_sem.at[panel * 2 + i]
+                amp_ref.at[panel, i], amps.at[panel, 0, i], amp_sem.at[panel * 2 + i]
             )
     local = {}
     for q in range(STAGES):
@@ -67,9 +69,9 @@
 
     barrier = pltpu.get_barrier_semaphore()
     along = [(pair, lax.rem(virt + step, 4)) for step in range(1, 4)]
-    for device in [first_up, first_down, second_up, second_down, sibling, opposite] + along:
+    for device in [first_up, first_down, first_far, second_up, second_down, sibling, opposite] + along:
         pl.semaphore_signal(barrier, inc=1, device_id=device, device_id_type=MESH)
-    pl.semaphore_wait(barrier, 9)
+    pl.semaphore_wait(barrier, 10)
 
     sent = []
 
@@ -92,10 +94,12 @@
         copy(q, number, target, target, sibling).wait_recv()
 
     def start_level(q, which, level):
-        send(q, RING1 + which, (OWN, OWN, level), (OWN, DOWN, level), first_up)
-        send(q, RING1 + which + 2, (OWN, OWN, level), (OWN, UP, level), first_down)
-        send(q, RING2 + which, (OWN, OWN, level), (DOWN, OWN, level), second_up)
-        send(q, RING2 + which + 2, (OWN, OWN, level), (UP, OWN, level), second_down)
+        here = (OWN, OWN, level)
+        send(q, RING1 + which * 3, here, (OWN, DOWN, level), first_up)
+        send(q, RING1 + which * 3 + 1, here, (OWN, UP, level), first_down)
+        send(q, RING1 + which * 3 + 2, here, (OWN, FAR, level), first_far)
+        send(q, RING2 + which * 2, here, (DOWN, OWN, level), second_up)
+        send(q, RING2 + which * 2 + 1, here, (UP, OWN, level), second_down)
 
     def begin(q):
         local[q].wait()
@@ -106,45 +110,43 @@
         receive(q, LEVEL, (OWN, OWN, 1 - h))
         start_level(q, 1, 1 - h)
 
-    near_two = pl.ds(UP, 2)
-
-    def near(q):
-        for which, level in enumerate((h, 1 - h)):
-            receive(q, RING1 + which, (OWN, DOWN, level))
-            receive(q, RING1 + which + 2, (OWN, UP, level))
-        send(q, RING1_FAR, (OWN, DOWN, h), (OWN, FAR, h), first_up)
-        send(q, RING1_FAR + 1, (OWN, UP, 1 - h), (OWN, FAR, 1 - h), first_down)
-        send(q, RING2_NEAR, (OWN, near_two), (DOWN, near_two), second_up)
-        send(q, RING2_NEAR + 1, (OWN, near_two), (UP, near_two), second_down)
-
-    def far(q):
-        receive(q, RING1_FAR, (OWN, FAR, h))
-        receive(q, RING1_FAR + 1, (OWN, FAR, 1 - h))
-        send(q, RING2_FAR, (OWN, FAR), (DOWN, FAR), second_up)
-        send(q, RING2_FAR + 1, (OWN, FAR), (UP, FAR), second_down)
-        send(q, CROSS, (OWN,), (OWN,), sibling)
-
-    every = pl.ds(0, 4)
-
-    def near_columns(q):
-        for way, (side, level, target) in enumerate(
-            ((DOWN, h, second_up), (UP, 1 - h, second_down))
-        ):
-            receive(q, RING2 + way * 2, (side, OWN, h))
-            receive(q, RING2 + way * 2 + 1, (side, OWN, 1 - h))
-            receive(q, RING2_NEAR + way, (side, near_two))
-            receive(q, RING2_FAR + way, (side, FAR))
-            send(q, ACROSS + way, (side, every, level), (FAR, every, level), target)
-            send(q, CROSS + 1 + way, (side,), (side,), sibling)
+    rest, every, near_two = pl.ds(UP, 3), pl.ds(OWN, 4), pl.ds(UP, 2)
+
+    def near(q, which):
+        level = (h, 1 - h)[which]
+        receive(q, RING1 + which * 3, (OWN, DOWN, level))
+        receive(q, RING1 + which * 3 + 1, (OWN, UP, level))
+        receive(q, RING1 + which * 3 + 2, (OWN, FAR, level))
+        send(q, RING2_REST + which * 2, (OWN, rest, level), (DOWN, rest, level), second_up)
+        send(q, RING2_REST + which * 2 + 1, (OWN, rest, level), (UP, rest, level), second_down)
+        if which:
+            send(q, CROSS, (OWN,), (OWN,), sibling)
+
+    def arrive(q, which, way):
+        side, level = (DOWN, UP)[way], (h, 1 - h)[which]
+        receive(q, RING2 + which * 2 + way, (side, OWN, level))
+        receive(q, RING2_REST + which * 2 + way, (side, rest, level))
+
+    def early_columns(q):
+        arrive(q, 0, 0)
+        send(q, ACROSS, (DOWN, every, h), (FAR, every, h), second_up)
+
+    def late_columns(q):
+        arrive(q, 1, 1)
+        send(q, ACROSS + 1, (UP, every, 1 - h), (FAR, every, 1 - h), second_down)
+        arrive(q, 0, 1)
+        arrive(q, 1, 0)
+        send(q, CROSS + 1, (near_two,), (near_two,), sibling)
 
     def far_columns(q):
         receive(q, ACROSS, (FAR, every, h))
         receive(q, ACROSS + 1, (FAR, every, 1 - h))
-        send(q, CROSS + 3, (FAR,), (FAR,), sibling)
+        send(q, CROSS + 2, (FAR,), (FAR,), sibling)
 
     def complete(q):
-        for number in range(4):
-            receive(q, CROSS + number, (number,))
+        receive(q, CROSS, (OWN,))
+        receive(q, CROSS + 1, (near_two,))
+        receive(q, CROSS + 2, (FAR,))
 
     def label(row, side):
         return irreps_ref[slab_ref[row, side]]
@@ -169,8 +171,8 @@
 
         def one(m):
             lanes = pl.ds(pl.multiple_of(m * LANES, LANES), LANES)
-            block_rows = plain[panel, i, :, lanes].astype(jnp.float32) * level
-            plain[panel, i, :, lanes] = block_rows.astype(jnp.bfloat16)
+            block_rows = amps[panel, 0, i, :, lanes].astype(jnp.float32) * level
+            amps[panel, 0, i, :, lanes] = block_rows.astype(jnp.bfloat16)
             turned[lanes, :] = block_rows.T
 
         unrolled(one, start, stop)
@@ -181,7 +183,7 @@
             odd = turned[pl.ds(2 * m + 1, TILE, stride=TILE), :]
             lanes = pl.ds(pl.multiple_of(m * LANES, LANES), LANES)
             both = jnp.concatenate([even, odd], axis=0).T
-            flipped[1 - panel, i, :, lanes] = both.astype(jnp.bfloat16)
+            amps[1 - panel, 1, i, :, lanes] = both.astype(jnp.bfloat16)
 
         unrolled(one, start, stop)
 
@@ -208,12 +210,8 @@
         distance = lax.rem(position - centre + 4, 4)
         return distance + distance // 2 - 2 * (distance // 3)
 
-    def multiply(q, rows_of):
-        for rows in rows_of:
-            partial[q, rows] = jnp.zeros((256, LANES), jnp.float32)
-
-        def step(n, carry):
-            panel, at_x = n // 4, lax.rem(n, 4)
+    def multiply(q, panel, kinds):
+        def step(at_x, carry):
             cells = []
             for level in range(2):
                 for at_y in range(4):
@@ -222,82 +220,113 @@
                     cells.append(panels[q, 1, near_x, near_y, level, panel])
             right = jnp.concatenate(cells, axis=0)
             lanes = pl.ds(pl.multiple_of(at_x * 1024, 1024), 1024)
-            for rows in rows_of:
-                source = (plain, flipped)[rows]
-                left = source[panel, :, :, lanes].reshape(256, 1024)
-                partial[q, rows] += jnp.dot(left, right, preferred_element_type=jnp.float32)
+            left = amps[panel, kinds, :, :, lanes]
+            count = left.shape[0]
+            left = left.reshape(count * 256, 1024)
+            product = jnp.dot(left, right, preferred_element_type=jnp.float32)
+            partial[q, kinds] += product.reshape(count, 256, LANES)
             return carry
 
-        lax.fori_loop(0, 8, step, 0)
+        lax.fori_loop(0, 4, step, 0)
+
+    both = pl.ds(0, 2)
 
     sums = []
 
+    def sum_copies(q, kind, source, device):
+        return [
+            pltpu.make_async_remote_copy(
+                src_ref=mine.at[q, kind],
+                dst_ref=theirs.at[source, kind],
+                send_sem=sum_send.at[n, q, kind],
+                recv_sem=sum_recv.at[n, source, kind],
+                device_id=device,
+                device_id_type=MESH,
+            )
+            for n, (mine, theirs) in enumerate(((coded, arrived), (scales, arrived_scales)))
+        ]
+
     def pass_on(q):
-        moved = pltpu.make_async_remote_copy(
-            src_ref=partial.at[q],
-            dst_ref=arrived.at[virt],
-            send_sem=sum_send.at[q],
-            recv_sem=sum_recv.at[virt],
-            device_id=(pair, blocks[q]),
-            device_id_type=MESH,
-        )
-        moved.start()
-        sums.append(moved)
-
+        for kind in (1, 0):
+            for i in range(2):
+                values = partial[q, kind, i * 128:(i + 1) * 128]
+                top = jnp.maximum(jnp.max(jnp.abs(values), axis=0, keepdims=True), 1e-33)
+                steps = jnp.round(values * (STEPS / top))
+                coded[q, kind, i * 128:(i + 1) * 128] = steps.astype(jnp.int32).astype(jnp.int16)
+                scales[q, kind, i] = jnp.broadcast_to(top * (1 / STEPS), (8, LANES))
+            for moved in sum_copies(q, kind, virt, (pair, blocks[q])):
+                moved.start()
+                sums.append(moved)
+
+    others = [lax.rem(virt + step, 4) for step in range(1, 4)]
+
+    def collect(kind, i):
+        here = slice(i * 128, (i + 1) * 128)
+        total = partial[3, kind, here]
+        for other in others:
+            steps = arrived[other, kind, here].astype(jnp.int32).astype(jnp.float32)
+            total += steps * arrived_scales[other, kind, i][0:1]
+        return total
+
+    partial[...] = jnp.zeros((STAGES, 2, 256, LANES), jnp.float32)
     for q in range(STAGES):
         begin(q)
+    prepare(4)
     begin_other(0)
+    near(0, 0)
+    prepare(1)
+    begin_other(1)
+    near(1, 0)
+    prepare(1)
+    begin_other(2)
+    near(2, 0)
+    begin_other(3)
+    near(3, 0)
     prepare(2)
-    begin_other(1)
-    near(0)
-    prepare(2)
-    far(0)
-    begin_other(2)
-    near(1)
-    prepare(2)
-    begin_other(3)
-    near_columns(0)
-    far(1)
-    prepare(2)
+    near(0, 1)
+    prepare(1)
+    near(1, 1)
+    early_columns(0)
+    prepare(1)
+    near(2, 1)
+    early_columns(1)
+    prepare(1)
+    near(3, 1)
+    early_columns(2)
+    prepare(1)
+    late_columns(0)
+    prepare(1)
+    early_columns(3)
+    prepare(1)
+    late_columns(1)
+    prepare(len(parts))
     far_columns(0)
-    near(2)
-    prepare(2)
-    near_columns(1)
-    far(2)
-    prepare(2)
+    late_columns(2)
     far_columns(1)
-    near(3)
-    prepare(len(parts))
     complete(0)
-    multiply(0, (1, 0))
+    multiply(0, 0, both)
+    late_columns(3)
+    multiply(0, 1, both)
     pass_on(0)
-    near_columns(2)
-    far(3)
+    far_columns(2)
     complete(1)
-    multiply(1, (1, 0))
+    multiply(1, 0, both)
+    far_columns(3)
+    multiply(1, 1, both)
     pass_on(1)
-    far_columns(2)
-    near_columns(3)
     complete(2)
-    multiply(2, (1, 0))
+    multiply(2, 0, both)
+    multiply(2, 1, both)
     pass_on(2)
-    far_columns(3)
     complete(3)
-    multiply(3, (1,))
-
-    others = [lax.rem(virt + step, 4) for step in range(1, 4)]
+    multiply(3, 0, pl.ds(1, 1))
+    multiply(3, 1, pl.ds(1, 1))
+
     for other in others:
-        pltpu.make_async_remote_copy(
-            src_ref=partial.at[0],
-            dst_ref=arrived.at[other],
-            send_sem=sum_send.at[0],
-            recv_sem=sum_recv.at[other],
-            device_id=(pair, other),
-            device_id_type=MESH,
-        ).wait_recv()
-    mirror_sum[...] = partial[3, 1] + (
-        arrived[others[0], 1] + arrived[others[1], 1] + arrived[others[2], 1]
-    )
+        for moved in sum_copies(3, 1, other, along[0]):
+            moved.wait_recv()
+    for i in range(2):
+        mirror_sum[i * 128:(i + 1) * 128] = collect(1, i)
     for which in range(2):
         for i in range(2):
             for j in range(2):
@@ -322,8 +351,13 @@
     tiles_in[pl.ds(pl.multiple_of(pair * 8, 8), 8), :] = tiles_out[
         pl.ds(pl.multiple_of((pair // 2) * 8, 8), 8), :
     ]
-    multiply(3, (0,))
-    partial[3, 0] += arrived[others[0], 0] + arrived[others[1], 0] + arrived[others[2], 0]
+    multiply(3, 0, pl.ds(0, 1))
+    multiply(3, 1, pl.ds(0, 1))
+    for other in others:
+        for moved in sum_copies(3, 0, other, along[0]):
+            moved.wait_recv()
+    for i in range(2):
+        partial[3, 0, i * 128:(i + 1) * 128] = collect(0, i)
 
     everything = pltpu.make_async_remote_copy(
         src_ref=tiles_in.at[pl.ds(0, 63 * 8)],
@@ -353,7 +387,7 @@
     smem = pl.BlockSpec(memory_space=pltpu.SMEM)
     anywhere = pl.BlockSpec(memory_space=pl.ANY)
     vmem = pl.BlockSpec(memory_space=pltpu.VMEM)
-    dma, f32, bf16 = pltpu.SemaphoreType.DMA, jnp.float32, jnp.bfloat16
+    dma, f32, bf16, i16 = pltpu.SemaphoreType.DMA, jnp.float32, jnp.bfloat16, jnp.int16
     return pl.pallas_call(
         kernel,
         out_shape=jax.ShapeDtypeStruct((2, 128, LANES), bf16),
@@ -361,11 +395,13 @@
         out_specs=vmem,
         scratch_shapes=[
             pltpu.VMEM((STAGES, 2, 4, 4, 2, 2, TILE, LANES), bf16),
-            pltpu.VMEM((2, 2, 128, 4096), bf16),
-            pltpu.VMEM((2, 2, 128, 4096), bf16),
+            pltpu.VMEM((2, 2, 2, 128, 4096), bf16),
             pltpu.VMEM((4096, 128), f32),
             pltpu.VMEM((STAGES, 2, 256, LANES), f32),
-            pltpu.VMEM((4, 2, 256, LANES), f32),
+            pltpu.VMEM((STAGES, 2, 256, LANES), i16),
+            pltpu.VMEM((STAGES, 2, 2, 8, LANES), f32),
+            pltpu.VMEM((4, 2, 256, LANES), i16),
+            pltpu.VMEM((4, 2, 2, 8, LANES), f32),
             pltpu.VMEM((256, LANES), f32),
             pltpu.VMEM((32 * 8, LANES), f32),
             pltpu.VMEM((64 * 8, LANES), f32),
@@ -374,8 +410,8 @@
             dma((4,)),
             dma((STAGES, COPIES)),
             dma((STAGES, COPIES)),
-            dma((STAGES,)),
-            dma((4,)),
+            dma((2, STAGES, 2)),
+            dma((2, 4, 2)),
             dma,
             dma,
         ],

time: 83.1 us -> 67.8 us (0.82)
  Pallas kernels: 76.4 us -> 61.1 us
    pallas_call x1, Pallas kernels: 76.4 us -> 61.1 us  [body(): pl.pallas_call(kernel, out_shape=jax.ShapeDtypeStruct((2, 128, LANES), bf...]
where the time goes in v3:
time: 67.8 us; the launch traced here: 67.7 us
  Pallas kernels  61.1 us (90%)
  local copies, waits for them, and re-layouts  6.54 us (10%)
    pallas_call x1, Pallas kernels, body(): pl.pallas_call(kernel, out_shape=jax.ShapeDtypeStruct((2, 128, LANES), bf...  61.1 us
    unnamed x9, local copies, waits for them, and re-layouts  6.54 us

profile of v3, /device:TPU:33, one launch (start us, length us, event | category | flops | bytes accessed | tf_op | source)
XLA Modules:
  0.0 67.7 jit_solution(2369094807338861628)
XLA Ops:
  0.0 0.8 %copy.7.slab_ref = s32[9,2]{1,0:T(8,128)S(1)} copy(s32[9,2]{0,1:T(2,128)} %param.9) | data formatting | bytes 144 | tf_op args[4]
  0.8 0.0 copy-start
  0.8 0.0 copy-start.1
  0.8 0.0 copy-start.2
  0.8 5.1 %copy.9 = bf16[2,128,2,4096]{3,1,0,2:T(8,128)(2,1)S(1)} copy(bf16[2,128,2,4096]{3,2,1,0:T(2,128)(2,1)} %param.5) | data formatting | bytes 8388608 | tf_op args[0]
  5.9 0.0 copy-done
  5.9 0.0 copy-done.1
  5.9 0.0 copy-done.2
  5.9 61.1 %shard_map.55 = bf16[2,128,128]{2,1,0:T(8,128)(2,1)S(1)} custom-call(s32[9,2]{1,0:T(8,128)S(1)} %copy.7.slab_ref, s32[16]{0:T(128)S(1)} %copy-done.2, s32[2,2]{1,0:T(2,128)S(1)} %copy-done.1, bf16[2,64,512]{2,1,0:T(8,128)(2,1)S(1)} %copy-done, bf16[2,2,128,4096]{3,2,1,0:T(8,128)(2,1)S(1)} %bitcast.3), custom_call_target="tpu_custom_call" | custom-call | flops 4294967296 | bytes 5242880 | tf_op jit(solution)/shard_map/pallas_call | solution.py:391
  67.1 0.6 copy.11
Async XLA Ops:
  0.8 5.1 %copy-start = (bf16[2,64,512]{2,1,0:T(8,128)(2,1)S(1)}, bf16[2,64,512]{2,1,0:T(8,128)(2,1)}, u32[]{:S(2)}) copy-start(bf16[2,64,512]{2,1,0:T(8,128)(2,1)} %own_ref.1) | copy-start | bytes 393220
  0.8 5.2 %copy-start.1 = (s32[2,2]{1,0:T(2,128)S(1)}, s32[2,2]{1,0:T(2,128)}, u32[]{:S(2)}) copy-start(s32[2,2]{1,0:T(2,128)} %screen_ref.1) | copy-start | bytes 52
  0.8 5.2 %copy-start.2 = (s32[16]{0:T(128)S(1)}, s32[16]{0:T(128)}, u32[]{:S(2)}) copy-start(s32[16]{0:T(128)} %irreps_ref.1) | copy-start | bytes 196

commit v4 on v3

--- a/solution.py
+++ b/solution.py
@@ -6,7 +6,8 @@
 from jax.sharding import PartitionSpec as P
 
 TILE = 64
-STAGES = 4
+STAGES = 2
+BLOCKS = 4
 LANES = 128
 MESH = pl.DeviceIdType.MESH
 
@@ -23,7 +24,7 @@
 def kernel(
     slab_ref, irreps_ref, screen_ref, own_ref, amp_ref, out_ref,
     panels, amps, turned, partial, coded, scales, arrived, arrived_scales, mirror_sum, tiles_out, tiles_in, result,
-    local_sem, amp_sem, send_sem, recv_sem, sum_send, sum_recv, tile_send, tile_recv,
+    local_sem, amp_sem, send_sem, recv_sem, sum_send, sum_recv, tile_send, tile_recv, own_sem,
 ):
     pair = lax.axis_index("pair")
     virt = lax.axis_index("virt")
@@ -58,12 +59,14 @@
                 amp_ref.at[panel, i], amps.at[panel, 0, i], amp_sem.at[panel * 2 + i]
             )
     local = {}
-    for q in range(STAGES):
-        columns = pl.ds(pl.multiple_of(blocks[q] * LANES, LANES), LANES)
-        local[q] = pltpu.make_async_copy(
-            own_ref.at[:, :, columns], panels.at[q, core, OWN, OWN, h], local_sem.at[q]
+    for n in range(BLOCKS):
+        columns = pl.ds(pl.multiple_of(blocks[n] * LANES, LANES), LANES)
+        local[n] = pltpu.make_async_copy(
+            own_ref.at[:, :, columns],
+            panels.at[n // 2, core, OWN, OWN, h, :, :, pl.ds(n % 2 * LANES, LANES)],
+            local_sem.at[n],
         )
-        local[q].start()
+        local[n].start()
     for load in loads.values():
         load.start()
 
@@ -102,7 +105,8 @@
         send(q, RING2 + which * 2 + 1, here, (UP, OWN, level), second_down)
 
     def begin(q):
-        local[q].wait()
+        local[2 * q].wait()
+        local[2 * q + 1].wait()
         send(q, LEVEL, (OWN, OWN, h), (OWN, OWN, h), opposite)
         start_level(q, 0, h)
 
@@ -149,7 +153,7 @@
         receive(q, CROSS + 2, (FAR,))
 
     def label(row, side):
-        return irreps_ref[slab_ref[row, side]]
+        return irreps_ref[slab_ref[side, row]]
 
     target_label = label(0, 0) + label(0, 1)
 
@@ -160,11 +164,11 @@
 
     def unrolled(one, start, stop):
         def step(m, carry):
-            for n in range(4):
-                one(m * 4 + n)
+            for n in range(8):
+                one(m * 8 + n)
             return carry
 
-        lax.fori_loop(start // 4, stop // 4, step, 0)
+        lax.fori_loop(start // 8, stop // 8, step, 0)
 
     def gate_part(panel, i, start, stop):
         level = gate(panel, i)
@@ -182,8 +186,8 @@
             even = turned[pl.ds(2 * m, TILE, stride=TILE), :]
             odd = turned[pl.ds(2 * m + 1, TILE, stride=TILE), :]
             lanes = pl.ds(pl.multiple_of(m * LANES, LANES), LANES)
-            both = jnp.concatenate([even, odd], axis=0).T
-            amps[1 - panel, 1, i, :, lanes] = both.astype(jnp.bfloat16)
+            both = jnp.concatenate([even, odd], axis=0).astype(jnp.bfloat16)
+            amps[1 - panel, 1, i, :, lanes] = both.T
 
         unrolled(one, start, stop)
 
@@ -211,23 +215,26 @@
         return distance + distance // 2 - 2 * (distance // 3)
 
     def multiply(q, panel, kinds):
-        def step(at_x, carry):
+        def step(n, carry):
             cells = []
-            for level in range(2):
-                for at_y in range(4):
-                    near_x, near_y = place(at_x, x), place(at_y, y)
-                    cells.append(panels[q, 0, near_y, near_x, level, panel])
-                    cells.append(panels[q, 1, near_x, near_y, level, panel])
+            for at_x in (2 * n, 2 * n + 1):
+                for level in range(2):
+                    for at_y in range(4):
+                        near_x, near_y = place(at_x, x), place(at_y, y)
+                        cells.append(panels[q, 0, near_y, near_x, level, panel])
+                        cells.append(panels[q, 1, near_x, near_y, level, panel])
             right = jnp.concatenate(cells, axis=0)
-            lanes = pl.ds(pl.multiple_of(at_x * 1024, 1024), 1024)
+            lanes = pl.ds(pl.multiple_of(n * 2048, 2048), 2048)
             left = amps[panel, kinds, :, :, lanes]
             count = left.shape[0]
-            left = left.reshape(count * 256, 1024)
+            left = left.reshape(count * 256, 2048)
             product = jnp.dot(left, right, preferred_element_type=jnp.float32)
-            partial[q, kinds] += product.reshape(count, 256, LANES)
+            for m in range(2):
+                part = product[:, m * LANES:(m + 1) * LANES]
+                partial[2 * q + m, kinds] += part.reshape(count, 256, LANES)
             return carry
 
-        lax.fori_loop(0, 4, step, 0)
+        lax.fori_loop(0, 2, step, 0)
 
     both = pl.ds(0, 2)
 
@@ -246,8 +253,8 @@
             for n, (mine, theirs) in enumerate(((coded, arrived), (scales, arrived_scales)))
         ]
 
-    def pass_on(q):
-        for kind in (1, 0):
+    def pass_on(q, kinds=(1, 0)):
+        for kind in kinds:
             for i in range(2):
                 values = partial[q, kind, i * 128:(i + 1) * 128]
                 top = jnp.maximum(jnp.max(jnp.abs(values), axis=0, keepdims=True), 1e-33)
@@ -268,59 +275,45 @@
             total += steps * arrived_scales[other, kind, i][0:1]
         return total
 
-    partial[...] = jnp.zeros((STAGES, 2, 256, LANES), jnp.float32)
-    for q in range(STAGES):
-        begin(q)
+    begin(0)
+    begin(1)
+    partial[...] = jnp.zeros((BLOCKS, 2, 256, LANES), jnp.float32)
     prepare(4)
     begin_other(0)
     near(0, 0)
-    prepare(1)
+    prepare(2)
     begin_other(1)
     near(1, 0)
-    prepare(1)
-    begin_other(2)
-    near(2, 0)
-    begin_other(3)
-    near(3, 0)
     prepare(2)
     near(0, 1)
     prepare(1)
     near(1, 1)
     early_columns(0)
-    prepare(1)
-    near(2, 1)
+    prepare(2)
     early_columns(1)
-    prepare(1)
-    near(3, 1)
-    early_columns(2)
-    prepare(1)
+    prepare(2)
     late_columns(0)
-    prepare(1)
-    early_columns(3)
-    prepare(1)
+    prepare(len(parts))
     late_columns(1)
-    prepare(len(parts))
     far_columns(0)
-    late_columns(2)
+    mirrors, directs = pl.ds(1, 1), pl.ds(0, 1)
+    complete(0)
+    multiply(0, 0, mirrors)
     far_columns(1)
-    complete(0)
-    multiply(0, 0, both)
-    late_columns(3)
-    multiply(0, 1, both)
-    pass_on(0)
-    far_columns(2)
+    multiply(0, 1, mirrors)
+    pass_on(0, (1,))
+    pass_on(1, (1,))
     complete(1)
-    multiply(1, 0, both)
-    far_columns(3)
-    multiply(1, 1, both)
-    pass_on(1)
-    complete(2)
-    multiply(2, 0, both)
-    multiply(2, 1, both)
-    pass_on(2)
-    complete(3)
-    multiply(3, 0, pl.ds(1, 1))
-    multiply(3, 1, pl.ds(1, 1))
+    multiply(1, 0, mirrors)
+    multiply(1, 1, mirrors)
+    pass_on(2, (1,))
+    multiply(0, 0, directs)
+    multiply(0, 1, directs)
+    pass_on(0, (0,))
+    pass_on(1, (0,))
+    multiply(1, 0, directs)
+    multiply(1, 1, directs)
+    pass_on(2, (0,))
 
     for other in others:
         for moved in sum_copies(3, 1, other, along[0]):
@@ -335,24 +328,33 @@
 
     def tile_copy(target):
         return pltpu.make_async_remote_copy(
-            src_ref=tiles_out.at[pl.ds(pl.multiple_of((target // 2) * 8, 8), 8)],
-            dst_ref=tiles_in.at[pl.ds(pl.multiple_of(pair * 8, 8), 8)],
+            src_ref=tiles_out.at[pl.ds(pl.multiple_of(target * 4, 4), 4)],
+            dst_ref=tiles_in.at[pl.ds(pl.multiple_of(pair * 4, 4), 4)],
             send_sem=tile_send,
             recv_sem=tile_recv,
             device_id=(target, virt),
             device_id_type=MESH,
         )
 
+    def away(n):
+        return n + n // 2 - 2 * (n // 3)
+
     def exchange(step, carry):
-        tile_copy(lax.rem(pair + step, 64)).start()
+        left = 63 - step
+        to_x = around(x, away(lax.rem(left // 8, 4)))
+        to_y = around(y, away(lax.rem(left // 2, 4)))
+        to_level = lax.rem(h + left // 32, 2)
+        to_core = lax.rem(core + lax.rem(left, 2), 2)
+        tile_copy(pair_index(to_x, to_level, to_y, to_core)).start()
         return carry
 
-    lax.fori_loop(1, 64, exchange, 0)
-    tiles_in[pl.ds(pl.multiple_of(pair * 8, 8), 8), :] = tiles_out[
-        pl.ds(pl.multiple_of((pair // 2) * 8, 8), 8), :
-    ]
-    multiply(3, 0, pl.ds(0, 1))
-    multiply(3, 1, pl.ds(0, 1))
+    lax.fori_loop(0, 63, exchange, 0)
+    own_tile = pltpu.make_async_copy(
+        tiles_out.at[pl.ds(pl.multiple_of(pair * 4, 4), 4)],
+        tiles_in.at[pl.ds(pl.multiple_of(pair * 4, 4), 4)],
+        own_sem,
+    )
+    own_tile.start()
     for other in others:
         for moved in sum_copies(3, 0, other, along[0]):
             moved.wait_recv()
@@ -360,18 +362,19 @@
         partial[3, 0, i * 128:(i + 1) * 128] = collect(0, i)
 
     everything = pltpu.make_async_remote_copy(
-        src_ref=tiles_in.at[pl.ds(0, 63 * 8)],
-        dst_ref=tiles_in.at[pl.ds(0, 63 * 8)],
+        src_ref=tiles_in.at[pl.ds(0, 63 * 4)],
+        dst_ref=tiles_in.at[pl.ds(0, 63 * 4)],
         send_sem=tile_send,
         recv_sem=tile_recv,
         device_id=(lax.rem(pair + 1, 64), virt),
         device_id_type=MESH,
     )
+    own_tile.wait()
     everything.wait_recv()
     for i in range(2):
         for j in range(2):
             direct = partial[3, 0, pl.ds(i * 128 + j, 64, stride=2), :]
-            mirrored = tiles_in[pl.ds(core * 4 + j * 2 + i, 64, stride=8), :]
+            mirrored = tiles_in[pl.ds(j * 2 + i, 64, stride=4), :]
             result[pl.ds(i * 128 + j, 64, stride=2), :] = 0.5 * (direct + mirrored)
     out_ref[...] = result[...].astype(jnp.bfloat16).reshape(2, 128, LANES)
 
@@ -394,24 +397,25 @@
         in_specs=[smem, smem, smem, anywhere, anywhere],
         out_specs=vmem,
         scratch_shapes=[
-            pltpu.VMEM((STAGES, 2, 4, 4, 2, 2, TILE, LANES), bf16),
+            pltpu.VMEM((STAGES, 2, 4, 4, 2, 2, TILE, 2 * LANES), bf16),
             pltpu.VMEM((2, 2, 2, 128, 4096), bf16),
             pltpu.VMEM((4096, 128), f32),
-            pltpu.VMEM((STAGES, 2, 256, LANES), f32),
-            pltpu.VMEM((STAGES, 2, 256, LANES), i16),
-            pltpu.VMEM((STAGES, 2, 2, 8, LANES), f32),
+            pltpu.VMEM((BLOCKS, 2, 256, LANES), f32),
+            pltpu.VMEM((BLOCKS, 2, 256, LANES), i16),
+            pltpu.VMEM((BLOCKS, 2, 2, 8, LANES), f32),
             pltpu.VMEM((4, 2, 256, LANES), i16),
             pltpu.VMEM((4, 2, 2, 8, LANES), f32),
             pltpu.VMEM((256, LANES), f32),
             pltpu.VMEM((32 * 8, LANES), f32),
-            pltpu.VMEM((64 * 8, LANES), f32),
+            pltpu.VMEM((64 * 4, LANES), f32),
             pltpu.VMEM((256, LANES), f32),
-            dma((STAGES,)),
+            dma((BLOCKS,)),
             dma((4,)),
             dma((STAGES, COPIES)),
             dma((STAGES, COPIES)),
-            dma((2, STAGES, 2)),
+            dma((2, BLOCKS, 2)),
             dma((2, 4, 2)),
+            dma,
             dma,
             dma,
         ],
@@ -421,7 +425,7 @@
         cost_estimate=pl.CostEstimate(
             flops=2 * 512 * 8192 * 512, bytes_accessed=5 << 20, transcendentals=0
         ),
-    )(slab_index, irreps, screen, integrals, rows)
+    )(slab_index.T, irreps, screen, integrals, rows)
 
 
 def solution(mesh):

time: 67.8 us -> 64.9 us (0.957)
  Pallas kernels: 61.1 us -> 59 us
  local copies, waits for them, and re-layouts: 6.54 us -> 5.78 us
    pallas_call x1, Pallas kernels: 61.1 us -> 59 us  [body(): pl.pallas_call(kernel, out_shape=jax.ShapeDtypeStruct((2, 128, LANES), bf...]
    unnamed x9 -> x10, local copies, waits for them, and re-layouts: 6.54 us -> 5.78 us
where the time goes in v4:
time: 64.9 us; the launch traced here: 64.8 us
  Pallas kernels  59 us (91%)
  local copies, waits for them, and re-layouts  5.78 us (9%)
    pallas_call x1, Pallas kernels, body(): pl.pallas_call(kernel, out_shape=jax.ShapeDtypeStruct((2, 128, LANES), bf...  59 us
    unnamed x10, local copies, waits for them, and re-layouts  5.78 us

profile of v4, /device:TPU:33, one launch (start us, length us, event | category | flops | bytes accessed | tf_op | source)
XLA Modules:
  0.0 64.8 jit_solution(3947872479963745501)
XLA Ops:
  0.0 0.0 copy-start
  0.0 0.0 copy-start.1
  0.0 0.0 copy-start.2
  0.0 0.0 copy-start.3
  0.0 5.1 %copy.8 = bf16[2,128,2,4096]{3,1,0,2:T(8,128)(2,1)S(1)} copy(bf16[2,128,2,4096]{3,2,1,0:T(2,128)(2,1)} %param.5) | data formatting | bytes 8388608 | tf_op args[0]
  5.2 0.0 copy-done
  5.2 0.0 copy-done.1
  5.2 0.0 copy-done.2
  5.2 0.0 copy-done.3
  5.2 59.0 %shard_map.55 = bf16[2,128,128]{2,1,0:T(8,128)(2,1)S(1)} custom-call(s32[2,9]{1,0:T(2,128)S(1)} %bitcast.5, s32[16]{0:T(128)S(1)} %copy-done.3, s32[2,2]{1,0:T(2,128)S(1)} %copy-done.2, bf16[2,64,512]{2,1,0:T(8,128)(2,1)S(1)} %copy-done, bf16[2,2,128,4096]{3,2,1,0:T(8,128)(2,1)S(1)} %bitcast.4), custom_call_target="tpu_custom_call" | custom-call | flops 4294967296 | bytes 5242880 | tf_op jit(solution)/shard_map/pallas_call | solution.py:394
  64.2 0.6 copy.10
Async XLA Ops:
  0.0 5.2 %copy-start = (bf16[2,64,512]{2,1,0:T(8,128)(2,1)S(1)}, bf16[2,64,512]{2,1,0:T(8,128)(2,1)}, u32[]{:S(2)}) copy-start(bf16[2,64,512]{2,1,0:T(8,128)(2,1)} %own_ref.1) | copy-start | bytes 393220
  0.0 5.2 %copy-start.1 = (s32[9,2]{0,1:T(2,128)S(1)}, s32[9,2]{0,1:T(2,128)}, u32[]{:S(2)}) copy-start(s32[9,2]{0,1:T(2,128)} %param.9) | copy-start | bytes 220
  0.0 5.2 %copy-start.2 = (s32[2,2]{1,0:T(2,128)S(1)}, s32[2,2]{1,0:T(2,128)}, u32[]{:S(2)}) copy-start(s32[2,2]{1,0:T(2,128)} %screen_ref.1) | copy-start | bytes 52
  0.0 5.2 %copy-start.3 = (s32[16]{0:T(128)S(1)}, s32[16]{0:T(128)}, u32[]{:S(2)}) copy-start(s32[16]{0:T(128)} %irreps_ref.1) | copy-start | bytes 196

commit v5 on v4

--- a/solution.py
+++ b/solution.py
@@ -278,18 +278,16 @@
     begin(0)
     begin(1)
     partial[...] = jnp.zeros((BLOCKS, 2, 256, LANES), jnp.float32)
-    prepare(4)
+    prepare(3)
+    near(0, 0)
+    near(1, 0)
     begin_other(0)
-    near(0, 0)
-    prepare(2)
     begin_other(1)
-    near(1, 0)
-    prepare(2)
+    prepare(3)
     near(0, 1)
-    prepare(1)
-    near(1, 1)
     early_columns(0)
     prepare(2)
+    near(1, 1)
     early_columns(1)
     prepare(2)
     late_columns(0)

time: 64.9 us -> 64.5 us (level)
  Pallas kernels: 59 us -> 58.3 us
where the time goes in v5:
time: 64.5 us; the launch traced here: 64.1 us
  Pallas kernels  58.3 us (90%)
  local copies, waits for them, and re-layouts  5.78 us (9%)
    pallas_call x1, Pallas kernels, body(): pl.pallas_call(kernel, out_shape=jax.ShapeDtypeStruct((2, 128, LANES), bf...  58.3 us
    unnamed x10, local copies, waits for them, and re-layouts  5.78 us

profile of v5, /device:TPU:33, one launch (start us, length us, event | category | flops | bytes accessed | tf_op | source)
XLA Modules:
  0.0 64.1 jit_solution(3087848948521782979)
XLA Ops:
  0.0 0.0 copy-start
  0.0 0.0 copy-start.1
  0.0 0.0 copy-start.2
  0.0 0.0 copy-start.3
  0.0 5.1 %copy.8 = bf16[2,128,2,4096]{3,1,0,2:T(8,128)(2,1)S(1)} copy(bf16[2,128,2,4096]{3,2,1,0:T(2,128)(2,1)} %param.5) | data formatting | bytes 8388608 | tf_op args[0]
  5.2 0.0 copy-done
  5.2 0.0 copy-done.1
  5.2 0.0 copy-done.2
  5.2 0.0 copy-done.3
  5.2 58.3 %shard_map.55 = bf16[2,128,128]{2,1,0:T(8,128)(2,1)S(1)} custom-call(s32[2,9]{1,0:T(2,128)S(1)} %bitcast.5, s32[16]{0:T(128)S(1)} %copy-done.3, s32[2,2]{1,0:T(2,128)S(1)} %copy-done.2, bf16[2,64,512]{2,1,0:T(8,128)(2,1)S(1)} %copy-done, bf16[2,2,128,4096]{3,2,1,0:T(8,128)(2,1)S(1)} %bitcast.4), custom_call_target="tpu_custom_call" | custom-call | flops 4294967296 | bytes 5242880 | tf_op jit(solution)/shard_map/pallas_call | solution.py:392
  63.5 0.6 copy.10
Async XLA Ops:
  0.0 5.2 %copy-start = (bf16[2,64,512]{2,1,0:T(8,128)(2,1)S(1)}, bf16[2,64,512]{2,1,0:T(8,128)(2,1)}, u32[]{:S(2)}) copy-start(bf16[2,64,512]{2,1,0:T(8,128)(2,1)} %own_ref.1) | copy-start | bytes 393220
  0.0 5.2 %copy-start.1 = (s32[9,2]{0,1:T(2,128)S(1)}, s32[9,2]{0,1:T(2,128)}, u32[]{:S(2)}) copy-start(s32[9,2]{0,1:T(2,128)} %param.9) | copy-start | bytes 220
  0.0 5.2 %copy-start.2 = (s32[2,2]{1,0:T(2,128)S(1)}, s32[2,2]{1,0:T(2,128)}, u32[]{:S(2)}) copy-start(s32[2,2]{1,0:T(2,128)} %screen_ref.1) | copy-start | bytes 52
  0.0 5.2 %copy-start.3 = (s32[16]{0:T(128)S(1)}, s32[16]{0:T(128)}, u32[]{:S(2)}) copy-start(s32[16]{0:T(128)} %irreps_ref.1) | copy-start | bytes 196

commit v6 on v5

--- a/solution.py
+++ b/solution.py
@@ -337,16 +337,18 @@
     def away(n):
         return n + n // 2 - 2 * (n // 3)
 
+    near_places = [around(y, step) * 2 + side for step in (2, 1, 3, 0) for side in (1 - core, core)]
+
     def exchange(step, carry):
-        left = 63 - step
-        to_x = around(x, away(lax.rem(left // 8, 4)))
-        to_y = around(y, away(lax.rem(left // 2, 4)))
-        to_level = lax.rem(h + left // 32, 2)
-        to_core = lax.rem(core + lax.rem(left, 2), 2)
-        tile_copy(pair_index(to_x, to_level, to_y, to_core)).start()
+        left = 7 - step
+        far_place = (around(x, away(lax.rem(left, 4))) * 2 + lax.rem(h + left // 4, 2)) * 8
+        for near_place in near_places:
+            tile_copy(far_place + near_place).start()
         return carry
 
-    lax.fori_loop(0, 63, exchange, 0)
+    lax.fori_loop(0, 7, exchange, 0)
+    for near_place in near_places[:-1]:
+        tile_copy((x * 2 + h) * 8 + near_place).start()
     own_tile = pltpu.make_async_copy(
         tiles_out.at[pl.ds(pl.multiple_of(pair * 4, 4), 4)],
         tiles_in.at[pl.ds(pl.multiple_of(pair * 4, 4), 4)],

time: 64.5 us -> 64.2 us (level)
  no operation moved by 1% of the time
where the time goes in v6:
time: 64.2 us; the launch traced here: 64.1 us
  Pallas kernels  58.3 us (91%)
  local copies, waits for them, and re-layouts  5.78 us (9%)
    pallas_call x1, Pallas kernels, body(): pl.pallas_call(kernel, out_shape=jax.ShapeDtypeStruct((2, 128, LANES), bf...  58.3 us
    unnamed x10, local copies, waits for them, and re-layouts  5.78 us

profile of v6, /device:TPU:33, one launch (start us, length us, event | category | flops | bytes accessed | tf_op | source)
XLA Modules:
  0.0 64.1 jit_solution(17329336648912845562)
XLA Ops:
  0.0 0.0 copy-start
  0.0 0.0 copy-start.1
  0.0 0.0 copy-start.2
  0.0 0.0 copy-start.3
  0.0 5.1 %copy.8 = bf16[2,128,2,4096]{3,1,0,2:T(8,128)(2,1)S(1)} copy(bf16[2,128,2,4096]{3,2,1,0:T(2,128)(2,1)} %param.5) | data formatting | bytes 8388608 | tf_op args[0]
  5.2 0.0 copy-done
  5.2 0.0 copy-done.1
  5.2 0.0 copy-done.2
  5.2 0.0 copy-done.3
  5.2 58.3 %shard_map.55 = bf16[2,128,128]{2,1,0:T(8,128)(2,1)S(1)} custom-call(s32[2,9]{1,0:T(2,128)S(1)} %bitcast.5, s32[16]{0:T(128)S(1)} %copy-done.3, s32[2,2]{1,0:T(2,128)S(1)} %copy-done.2, bf16[2,64,512]{2,1,0:T(8,128)(2,1)S(1)} %copy-done, bf16[2,2,128,4096]{3,2,1,0:T(8,128)(2,1)S(1)} %bitcast.4), custom_call_target="tpu_custom_call" | custom-call | flops 4294967296 | bytes 5242880 | tf_op jit(solution)/shard_map/pallas_call | solution.py:394
  63.5 0.6 copy.10
Async XLA Ops:
  0.0 5.2 %copy-start = (bf16[2,64,512]{2,1,0:T(8,128)(2,1)S(1)}, bf16[2,64,512]{2,1,0:T(8,128)(2,1)}, u32[]{:S(2)}) copy-start(bf16[2,64,512]{2,1,0:T(8,128)(2,1)} %own_ref.1) | copy-start | bytes 393220
  0.0 5.2 %copy-start.1 = (s32[9,2]{0,1:T(2,128)S(1)}, s32[9,2]{0,1:T(2,128)}, u32[]{:S(2)}) copy-start(s32[9,2]{0,1:T(2,128)} %param.9) | copy-start | bytes 220
  0.0 5.2 %copy-start.2 = (s32[2,2]{1,0:T(2,128)S(1)}, s32[2,2]{1,0:T(2,128)}, u32[]{:S(2)}) copy-start(s32[2,2]{1,0:T(2,128)} %screen_ref.1) | copy-start | bytes 52
  0.0 5.2 %copy-start.3 = (s32[16]{0:T(128)S(1)}, s32[16]{0:T(128)}, u32[]{:S(2)}) copy-start(s32[16]{0:T(128)} %irreps_ref.1) | copy-start | bytes 196
